TPU v7x, 128 devices: a whole 4x4x4 slice. The times are simulated.
128 devices in a mesh: tm: 8 (over x_lo, z), patch: 16 (over x_hi, y, core).
Axes of the slice: x: 4 (x_hi: 2, x_lo: 2; x = x_hi * 2 + x_lo), y: 4, z: 4, core: 2. Of those that a mesh axis runs over, the one named last changes fastest.
Arguments:
- video_tokens: float32 [128, 256, 768], P('tm', 'patch'), may hold values from -6 to 6
- cotangent: float32 [128, 256, 768], P('tm', 'patch'), may hold values from -6 to 6
- weights: float32 [2, 768, 3072], replicated, may hold values from -0.21650635 to 0.21650635, as said below
Outputs:
- mixed: float32 [128, 256, 768], P('tm', 'patch')
- grad_input: float32 [128, 256, 768], P('tm', 'patch')
- grad_weights: float32 [2, 768, 3072], P(None, None, ('tm', 'patch'))
Inputs may be any that keep to these rules, and one draw needn't show every extreme that they name: `weights`: entries scaled by 768 ** -0.5, one over the root of the fan-in.
All inputs are finite; a program needn't handle non-finite values.
Results may differ from a plain program's by a relative error of at most 0.0007.
Values sent between devices are 32-bit elements; how exact they have to be, the bound alone decides.
A program may use at most 192 MiB of HBM per device.

v0:
```python
import math

import jax
import jax.numpy as jnp
from jax import lax
from jax.sharding import PartitionSpec as P

HEADS = 12
PATCHES = 256


HIGH = lax.Precision.HIGHEST


def normalize(inputs):
    center = inputs - jnp.mean(inputs, axis=-1, keepdims=True)
    spread = jnp.mean(center * center, axis=-1, keepdims=True)
    return center * lax.rsqrt(spread + 1e-05)


def attend(inputs, weight, layout_kind):
    width = inputs.shape[-1]
    head_dim = width // HEADS
    normed = normalize(inputs)
    project = jnp.einsum("abd,df->abf", normed, weight[:, : 3 * width], precision=HIGH)
    shape = inputs.shape[:2] + (HEADS, head_dim)
    queries = project[..., :width].reshape(shape)
    keys_all = project[..., width : 2 * width].reshape(shape)
    values = project[..., 2 * width :].reshape(shape)
    if layout_kind == "lg":
        scores = jnp.einsum("lghe,mghe->ghlm", queries, keys_all, precision=HIGH)
    else:
        scores = jnp.einsum("glhe,gmhe->ghlm", queries, keys_all, precision=HIGH)
    scores = scores * (1.0 / math.sqrt(head_dim))
    row_max = jnp.max(scores, axis=-1, keepdims=True)
    lifted = jnp.exp(scores - row_max)
    probs = lifted / jnp.sum(lifted, axis=-1, keepdims=True)
    if layout_kind == "lg":
        context = jnp.einsum("ghlm,mghe->lghe", probs, values, precision=HIGH)
    else:
        context = jnp.einsum("ghlm,gmhe->glhe", probs, values, precision=HIGH)
    merged = context.reshape(inputs.shape)
    return jnp.einsum("abd,df->abf", merged, weight[:, 3 * width :], precision=HIGH)


def temporal_branch(inputs, weight):
    return attend(inputs, weight, "lg")


def spatial_branch(inputs, weight):
    return attend(inputs, weight, "gl")


def on_device(video_tokens, cotangent, weights):
    track_in = lax.all_to_all(video_tokens, "tm", split_axis=1, concat_axis=0, tiled=True)
    temporal_out, temporal_pull = jax.vjp(temporal_branch, track_in, weights[0])
    middle_track = track_in + temporal_out
    middle_home = lax.all_to_all(middle_track, "tm", split_axis=0, concat_axis=1, tiled=True)
    middle_frame = lax.all_to_all(middle_home, "patch", split_axis=0, concat_axis=1, tiled=True)
    spatial_out, spatial_pull = jax.vjp(spatial_branch, middle_frame, weights[1])
    mixed = lax.all_to_all(
        middle_frame + spatial_out, "patch", split_axis=1, concat_axis=0, tiled=True
    )
    total_tokens = middle_track.shape[0] * PATCHES
    factor = 1.0 / math.sqrt(total_tokens)
    grad_frame = lax.all_to_all(cotangent, "patch", split_axis=0, concat_axis=1, tiled=True)
    spatial_input_grad, spatial_weight_grad = spatial_pull(grad_frame)
    middle_grad_frame = grad_frame + spatial_input_grad
    middle_grad_home = lax.all_to_all(
        middle_grad_frame, "patch", split_axis=1, concat_axis=0, tiled=True
    )
    middle_grad_track = lax.all_to_all(
        middle_grad_home, "tm", split_axis=1, concat_axis=0, tiled=True
    )
    temporal_input_grad, temporal_weight_grad = temporal_pull(middle_grad_track)
    grad_input = lax.all_to_all(
        middle_grad_track + temporal_input_grad, "tm", split_axis=0, concat_axis=1, tiled=True
    )
    stacked = jnp.stack([temporal_weight_grad, spatial_weight_grad])
    grad_weights = (
        lax.psum_scatter(stacked, ("tm", "patch"), scatter_dimension=2, tiled=True) * factor
    )
    return (mixed, grad_input, grad_weights)


def solution(mesh):
    placed = (P("tm", "patch", None), P("tm", "patch", None), P())
    return jax.shard_map(
        on_device,
        mesh=mesh,
        in_specs=placed,
        out_specs=(P("tm", "patch", None), P("tm", "patch", None), P(None, None, ("tm", "patch"))),
        check_vma=False,
    )
```

profile of v0, /device:TPU:1, one launch (start us, length us, event | category | flops | bytes accessed | tf_op | source)
XLA Modules:
  0.0 544.7 jit_solution(17909727988491595841)
XLA Ops:
  9.6 6.8 %all-to-all-start = ((f32[16,16,768]{2,0,1:T(8,128)}), f32[16,16,768]{2,0,1:T(8,128)S(1)}, u32[]{:S(2)}, u32[]{:S(2)}) async-start(f32[16,16,768]{2,0,1:T(8,128)} %copy.161), calls=%async_computation | async-start | bytes 1572864 | tf_op jit(solution)/shard_map/all_to_all | solution.py:55
  16.4 12.4 %slice_bitcast_fusion = (f32[768,3072]{1,0:T(8,128)}, f32[768,3072]{1,0:T(8,128)}) fusion(f32[2,768,3072]{2,1,0:T(8,128)} %param.5), kind=kLoop, calls=%fused_computation.3 | loop fusion | bytes 37748736 | tf_op jit(solution)/shard_map/squeeze | solution.py:60
  29.6 8.6 %fusion.5 = f32[128,2,2304]{2,0,1:T(8,128)S(1)} fusion(f32[768,3072]{1,0:T(8,128)} %get-tuple-element.32, f32[128,2,768]{2,0,1:T(8,128)S(1)} %bitcast_subtract_fusion.1, f32[128,2]{0,1:T(2,128)S(1)} %rsqrt.21), kind=kOutput, calls=%fused_computation.11 | convolution fusion | flops 5436014592 | bytes 10224640 | tf_op jit(solution)/shard_map/jvp(abd,df->abf)/dot_general | solution.py:25
  53.7 16.1 %all_to_all.123 = f32[128,2,768]{2,1,0:T(2,128)} all-to-all(f32[128,2,768]{2,1,0:T(2,128)S(1)} %copy.168), channel_id=1, replica_groups=mesh['tm'=8,'patch'=16] {'tm'}, dimensions={0} | all-to-all | bytes 1572864 | tf_op jit(solution)/shard_map/all_to_all | solution.py:58
  69.8 9.7 %all-to-all-start.4 = ((f32[16,16,768]{2,1,0:T(8,128)}), f32[16,16,768]{2,1,0:T(8,128)S(1)}, u32[]{:S(2)}, u32[]{:S(2)}) async-start(f32[16,16,768]{2,1,0:T(8,128)} %param.4), calls=%async_computation.4 | async-start | bytes 1572864 | tf_op jit(solution)/shard_map/all_to_all | solution.py:66
  82.1 11.8 %all-to-all-done.4 = f32[16,16,768]{2,1,0:T(8,128)S(1)} async-done(((f32[16,16,768]{2,1,0:T(8,128)}), f32[16,16,768]{2,1,0:T(8,128)S(1)}, u32[]{:S(2)}, u32[]{:S(2)}) %all-to-all-start.4) | async-done | bytes 786464 | tf_op jit(solution)/shard_map/all_to_all | solution.py:66
  107.1 6.4 %all-to-all-done.2 = f32[16,16,768]{2,1,0:T(8,128)S(1)} async-done(((f32[16,16,768]{2,1,0:T(8,128)}), f32[16,16,768]{2,1,0:T(8,128)S(1)}, u32[]{:S(2)}, u32[]{:S(2)}) %all-to-all-start.2) | async-done | bytes 786464 | tf_op jit(solution)/shard_map/all_to_all | solution.py:59
  114.5 8.3 %fusion.6 = f32[1,256,2304]{2,1,0:T(8,128)S(1)} fusion(f32[768,3072]{1,0:T(8,128)} %get-tuple-element.31, f32[256,768]{1,0:T(8,128)S(1)} %bitcast_subtract_fusion, f32[256]{0:T(256)S(1)} %rsqrt.22), kind=kOutput, calls=%fused_computation.13 | convolution fusion | flops 5436014592 | bytes 10224640 | tf_op jit(solution)/shard_map/jvp(abd,df->abf)/dot_general | solution.py:25
  131.1 4.3 multiply_reduce_fusion.1
  151.2 12.3 %multiply_reduce_fusion.4 = (f32[256]{0:T(256)S(1)}, f32[256,768]{1,0:T(8,128)S(1)}) fusion(f32[16,16,768]{2,1,0:T(8,128)S(1)} %all-to-all-done.2, f32[256]{0:T(256)S(1)} %div.102, f32[768,3072]{1,0:T(8,128)S(1)} %bitcast.165, f32[1,256,768]{1,2,0:T(8,128)S(1)} %bitcast.186, f32[1,256,768]{1,2,0:T(8,128)S(1)} %bitcast.188, f32[1,256,768]{1,2,0:T(8,128)S(1)} %bitcast.200), kind=kOutput, calls=%fused_computation.72 | convolution fusion | flops 5437587456 | bytes 11012096 | tf_op jit(solution)/shard_map/transpose(jvp(abd,df->abf))/dot_general | solution.py:25
  165.7 4.9 all-to-all-start.5
  170.6 15.1 %fusion.9 = f32[768,2304]{1,0:T(8,128)} fusion(f32[1,256,768]{1,2,0:T(8,128)} %bitcast.187, f32[1,256,768]{1,2,0:T(8,128)} %bitcast.189, f32[1,256,768]{1,2,0:T(8,128)} %bitcast.201, f32[1,256,1,1,1,1,768]{6,1,5,4,3,2,0:T(8,128)S(1)} %bitcast.166, f32[256]{0:T(256)S(1)} %rsqrt.22, f32[256]{0:T(256)S(1)} %div.102), kind=kOutput, calls=%fused_computation.21 | convolution fusion | flops 5437390848 | bytes 10225664 | tf_op jit(solution)/shard_map/transpose(jvp(abd,df->abf))/dot_general | solution.py:25
  196.2 4.8 fusion.79
  201.1 8.7 %add_bitcast_fusion = f32[1,768,3072]{2,1,0:T(8,128)} fusion(f32[768,2304]{1,0:T(8,128)} %fusion.9, f32[768,768]{1,0:T(8,128)} %fusion.79), kind=kLoop, calls=%fused_computation.1 | loop fusion | flops 2359296 | bytes 18874368 | tf_op jit(solution)/shard_map/stack | solution.py:79
  237.1 4.8 convolution_bitcast_fusion.1
  241.9 8.2 %convolution_bitcast_fusion = f32[768,2304]{1,0:T(8,128)} fusion(f32[128,2,768]{2,0,1:T(8,128)S(1)} %copy-done.14, f32[128,2,768]{2,0,1:T(8,128)S(1)} %copy-done.15, f32[128,2,768]{2,0,1:T(8,128)S(1)} %copy-done.16, f32[128,2,768]{2,0,1:T(8,128)S(1)} %copy-done.8, f32[128,2]{0,1:T(2,128)S(1)} %rsqrt.21), kind=kOutput, calls=%fused_computation.12 | convolution fusion | flops 5437194240 | bytes 10224640 | tf_op jit(solution)/shard_map/transpose(jvp(abd,df->abf))/dot_general | solution.py:25
  250.0 8.7 %add_bitcast_fusion.1 = f32[1,768,3072]{2,1,0:T(8,128)} fusion(f32[768,2304]{1,0:T(8,128)} %convolution_bitcast_fusion, f32[768,768]{1,0:T(8,128)} %convolution_bitcast_fusion.1), kind=kLoop, calls=%fused_computation.2 | loop fusion | flops 2359296 | bytes 18874368 | tf_op jit(solution)/shard_map/stack | solution.py:79
  258.8 13.0 %pad_maximum_fusion = f32[2,768,3072]{2,1,0:T(8,128)} fusion(f32[1,768,3072]{2,1,0:T(8,128)} %add_bitcast_fusion, f32[1,768,3072]{2,1,0:T(8,128)} %add_bitcast_fusion.1), kind=kLoop, calls=%fused_computation | loop fusion | flops 4718592 | bytes 37748736 | tf_op jit(solution)/shard_map/stack | solution.py:79
  271.8 28.2 %copy.197 = f32[2,768,3072]{1,0,2:T(2,128)} copy(f32[2,768,3072]{2,1,0:T(8,128)} %pad_maximum_fusion) | data formatting | bytes 37748736 | tf_op jit(solution)/shard_map/stack | solution.py:79
  305.8 7.3 %all-to-all-start.3 = ((f32[1,256,768]{2,0,1:T(1,128)}), f32[1,256,768]{2,0,1:T(1,128)}, u32[]{:S(2)}, u32[]{:S(2)}) async-start(f32[1,256,768]{2,0,1:T(1,128)} %copy.181), calls=%async_computation.3 | async-start | bytes 1572864 | tf_op jit(solution)/shard_map/all_to_all | solution.py:61
  313.1 9.5 %multiply_reduce_fusion.3 = (f32[128,2]{0,1:T(2,128)S(1)}, f32[128,2,768]{2,0,1:T(8,128)S(1)}) fusion(f32[128,2,768]{2,0,1:T(8,128)S(1)} %copy-done.8, f32[768,3072]{1,0:T(8,128)} %get-tuple-element.32, f32[128,2,768]{2,0,1:T(8,128)} %copy.193, f32[128,2,768]{2,0,1:T(8,128)} %copy.191, f32[128,2,768]{2,0,1:T(8,128)} %copy.189), kind=kOutput, calls=%fused_computation.66 | convolution fusion | flops 5437390848 | bytes 11011072 | tf_op jit(solution)/shard_map/transpose(jvp(abd,df->abf))/dot_general | solution.py:25
  324.6 6.8 %all-to-all-done.3 = f32[1,256,768]{2,0,1:T(1,128)} async-done(((f32[1,256,768]{2,0,1:T(1,128)}), f32[1,256,768]{2,0,1:T(1,128)}, u32[]{:S(2)}, u32[]{:S(2)}) %all-to-all-start.3) | async-done | bytes 786464 | tf_op jit(solution)/shard_map/all_to_all | solution.py:61
  337.8 12.2 %all-to-all-done.7 = f32[128,2,768]{2,1,0:T(2,128)S(1)} async-done(((f32[128,2,768]{2,1,0:T(2,128)}), f32[128,2,768]{2,1,0:T(2,128)S(1)}, u32[]{:S(2)}, u32[]{:S(2)}) %all-to-all-start.7) | async-done | bytes 786464 | tf_op jit(solution)/shard_map/all_to_all | solution.py:76
  351.6 184.2 %all-reduce.13.cloned.1.call-done = f32[2,768,3072]{1,0,2:T(2,128)} async-done(((f32[2,768,3072]{1,0,2:T(2,128)}), f32[2,768,3072]{1,0,2:T(2,128)}) %all-reduce.13.cloned.1.call-update) | async-done | bytes 18874384
  (150 shorter events, 116.6 us)
Async XLA Ops:
  9.6 19.2 %all-to-all-start = ((f32[16,16,768]{2,0,1:T(8,128)}), f32[16,16,768]{2,0,1:T(8,128)S(1)}, u32[]{:S(2)}, u32[]{:S(2)}) async-start(f32[16,16,768]{2,0,1:T(8,128)} %copy.161), calls=%async_computation | async-start | bytes 1572864 | tf_op jit(solution)/shard_map/all_to_all | solution.py:55
  29.6 8.6 %copy-start.7 = (f32[128,2,768]{2,0,1:T(8,128)}, f32[128,2,768]{2,0,1:T(8,128)S(1)}, u32[]{:S(2)}) copy-start(f32[128,2,768]{2,0,1:T(8,128)S(1)} %bitcast_subtract_fusion.1) | copy-start | bytes 2359300
  41.8 5.3 copy-start.9
  69.8 24.1 %all-to-all-start.4 = ((f32[16,16,768]{2,1,0:T(8,128)}), f32[16,16,768]{2,1,0:T(8,128)S(1)}, u32[]{:S(2)}, u32[]{:S(2)}) async-start(f32[16,16,768]{2,1,0:T(8,128)} %param.4), calls=%async_computation.4 | async-start | bytes 1572864 | tf_op jit(solution)/shard_map/all_to_all | solution.py:66
  94.8 18.8 %all-to-all-start.2 = ((f32[16,16,768]{2,1,0:T(8,128)}), f32[16,16,768]{2,1,0:T(8,128)S(1)}, u32[]{:S(2)}, u32[]{:S(2)}) async-start(f32[16,16,768]{2,1,0:T(8,128)} %copy.171), calls=%async_computation.2 | async-start | bytes 1572864 | tf_op jit(solution)/shard_map/all_to_all | solution.py:59
  131.1 4.9 copy-start.23
  131.1 4.9 copy-start.25
  135.5 12.2 %copy-start = (f32[12,256,256]{1,2,0:T(8,128)}, f32[12,256,256]{1,2,0:T(8,128)S(1)}, u32[]{:S(2)}) copy-start(f32[12,256,256]{1,2,0:T(8,128)S(1)} %get-tuple-element.44) | copy-start | bytes 9437188
  141.2 10.0 %slice-start = ((s8[9437184]{0:T(1024)(128)(4,1)}), s8[4194304]{0:T(1024)(128)(4,1)S(1)}, s32[]{:S(2)}) async-start(s8[9437184]{0:T(1024)(128)(4,1)} %bitcast.164), calls=%async_computation.9 | async-start | bytes 8388608
  143.9 7.3 %copy-start.17 = (f32[12,256,64]{1,2,0:T(8,128)}, f32[12,256,64]{1,2,0:T(8,128)S(1)}, u32[]{:S(2)}) copy-start(f32[12,256,64]{1,2,0:T(8,128)S(1)} %fusion.14) | copy-start | bytes 2359300
  143.9 7.3 %slice-start.1 = ((s8[9437184]{0:T(1024)(128)(4,1)}), s8[4194304]{0:T(1024)(128)(4,1)S(1)}, s32[]{:S(2)}) async-start(s8[9437184]{0:T(1024)(128)(4,1)} %bitcast.164), calls=%async_computation.10 | async-start | bytes 8388608
  151.1 12.4 %copy-start.20 = (f32[12,64,256]{2,1,0:T(8,128)}, f32[12,64,256]{2,1,0:T(8,128)S(1)}, u32[]{:S(2)}) copy-start(f32[12,64,256]{2,1,0:T(8,128)S(1)} %fusion.45) | copy-start | bytes 2359300
  151.2 12.7 %copy-start.4 = (f32[16,16,768]{2,1,0:T(8,128)S(1)}, f32[16,16,768]{2,1,0:T(8,128)}, u32[]{:S(2)}) copy-start(f32[16,16,768]{2,1,0:T(8,128)} %copy-done.2) | copy-start | bytes 2359300
  165.7 23.5 %all-to-all-start.5 = ((f32[1,256,768]{2,0,1:T(1,128)}), f32[1,256,768]{2,0,1:T(1,128)}, u32[]{:S(2)}, u32[]{:S(2)}) async-start(f32[1,256,768]{2,0,1:T(1,128)} %copy.185), calls=%async_computation.5 | async-start | bytes 1572864 | tf_op jit(solution)/shard_map/all_to_all | solution.py:69
  170.6 15.1 %copy-start.1 = (f32[12,256,256]{1,2,0:T(8,128)S(1)}, f32[12,256,256]{1,2,0:T(8,128)}, u32[]{:S(2)}) copy-start(f32[12,256,256]{1,2,0:T(8,128)} %copy-done) | copy-start | bytes 9437188
  170.6 15.1 %copy-start.24 = (f32[1,256,768]{1,2,0:T(8,128)S(1)}, f32[1,256,768]{1,2,0:T(8,128)}, u32[]{:S(2)}) copy-start(f32[1,256,768]{1,2,0:T(8,128)} %copy.177) | copy-start | bytes 2359300
  191.8 18.0 %all-to-all-start.6 = ((f32[16,16,768]{2,0,1:T(8,128)}), f32[16,16,768]{2,0,1:T(8,128)}, u32[]{:S(2)}, u32[]{:S(2)}) async-start(f32[16,16,768]{2,0,1:T(8,128)} %copy.186), calls=%async_computation.6 | async-start | bytes 1572864 | tf_op jit(solution)/shard_map/all_to_all | solution.py:72
  196.0 339.8 %all-reduce.13.cloned.1.call-start = ((), (), s32[]{:S(2)}) async-start(), calls=%async_computation.8 | async-start | bytes 37748736
  209.7 5.3 copy-start.22
  211.0 7.0 %copy-start.5 = (f32[8,16,2,768]{3,1,0,2:T(8,128)}, f32[8,16,2,768]{3,1,0,2:T(8,128)S(1)}, u32[]{:S(2)}) copy-start(f32[8,16,2,768]{3,1,0,2:T(8,128)S(1)} %copy.187) | copy-start | bytes 2359300
  230.0 7.1 %copy-start.6 = (f32[8,16,2,768]{3,1,0,2:T(8,128)S(1)}, f32[8,16,2,768]{3,1,0,2:T(8,128)}, u32[]{:S(2)}) copy-start(f32[8,16,2,768]{3,1,0,2:T(8,128)} %copy-done.5) | copy-start | bytes 2359300
  234.7 7.2 %copy-start.8 = (f32[128,2,768]{2,0,1:T(8,128)S(1)}, f32[128,2,768]{2,0,1:T(8,128)}, u32[]{:S(2)}) copy-start(f32[128,2,768]{2,0,1:T(8,128)} %copy-done.7) | copy-start | bytes 2359300
  305.8 25.6 %all-to-all-start.3 = ((f32[1,256,768]{2,0,1:T(1,128)}), f32[1,256,768]{2,0,1:T(1,128)}, u32[]{:S(2)}, u32[]{:S(2)}) async-start(f32[1,256,768]{2,0,1:T(1,128)} %copy.181), calls=%async_computation.3 | async-start | bytes 1572864 | tf_op jit(solution)/shard_map/all_to_all | solution.py:61
  331.4 18.6 %all-to-all-start.7 = ((f32[128,2,768]{2,1,0:T(2,128)}), f32[128,2,768]{2,1,0:T(2,128)S(1)}, u32[]{:S(2)}, u32[]{:S(2)}) async-start(f32[128,2,768]{2,1,0:T(2,128)} %copy.194), calls=%async_computation.7 | async-start | bytes 1572864 | tf_op jit(solution)/shard_map/all_to_all | solution.py:76
  (13 other events, 41.9 us)
Sparse Core Ops, SparseCore 0:
  300.1 235.6 all-reduce.12
where the time goes:
time: 555 us; the launch traced here: 545 us
  waiting for transfers between devices  221 us (40%)
  matrix products  128 us (23%)
  local copies, waits for them, and re-layouts  86.9 us (16%)
  starting transfers between devices  41.7 us (8%)
  other arithmetic  35.8 us (6%)
  blocking collectives  16.1 us (3%)
  between operations  15 us (3%)
    unnamed x2, waiting for transfers between devices  184 us
    dot_general x6, matrix products, attend(): jnp.einsum('abd,df->abf', normed, weight[:, :3 * width], precision=HIGH)  61.9 us
    another operation x3, other arithmetic, on_device(): stacked = jnp.stack([temporal_weight_grad, spatial_weight_grad])  30.4 us
    another operation x1, local copies, waits for them, and re-layouts, on_device(): stacked = jnp.stack([temporal_weight_grad, spatial_weight_grad])  28.2 us
    dot_general x6, matrix products, attend(): jnp.einsum('abd,df->abf', merged, weight[:, 3 * width:], precision=HIGH)  24.8 us
    all_to_all x1, blocking collectives, on_device(): lax.all_to_all(middle_track, 'tm', split_axis=0, concat_axis=1, tiled=True)  16.1 us
    squeeze x1, local copies, waits for them, and re-layouts, on_device(): weights[1]  12.4 us
    all_to_all x1, waiting for transfers between devices, on_device(): lax.all_to_all(middle_grad_track + temporal_input_grad, 'tm', split_axis=...  12.2 us
  transfers between devices with their start and end apart: 8, of which 5 were waited for; matrix products, arithmetic and copies ran while one was open for 14% of the time, Pallas kernels for 0%

commit v1 on v0

v1 whole, which is shorter than its diff:
```python
import math

import jax
import jax.numpy as jnp
from jax import lax
from jax.experimental import pallas as pl
from jax.experimental.pallas import tpu as pltpu
from jax.sharding import PartitionSpec as P

VMEM_LIMIT = 62 * 2**20
MESH = pl.DeviceIdType.MESH


def position():
    tm = lax.axis_index("tm")
    patch = lax.axis_index("patch")
    coords = (
        (patch // 8) * 2 + tm // 4,
        (patch // 2) % 4,
        tm % 4,
    )
    return tm, patch, patch % 2, coords


def flip(value, bits):
    result = value
    for bit in (1, 2, 4, 8):
        if bits & bit:
            has = (value // bit) % 2
            result = result + bit - 2 * bit * has
    return result


def partner(tm, patch, axis, mask):
    if axis == 0:
        return flip(tm, 4 * (mask & 1)), flip(patch, 8 * (mask >> 1))
    if axis == 1:
        return tm, flip(patch, 2 * mask)
    return flip(tm, mask), patch


class ScatterSum:
    def __init__(self, grads, core_in, ins, send, recv):
        self.grads, self.core_in, self.ins, self.send, self.recv = grads, core_in, ins, send, recv
        self.tm, self.patch, self.core, self.coords = position()

    def order(self, piece):
        turn = (piece // 2) % 3
        masks = (1, 3) if piece % 2 == 0 else (3, 1)
        return [(turn + k) % 3 for k in range(3)], masks

    def view(self, piece, stage, where):
        axes, _ = self.order(piece)
        index = [slice(None)] * 3
        for axis in axes[:stage]:
            index[axis] = self.coords[axis]
        index[axes[stage]] = where
        return self.grads.at[(self.core, piece) + tuple(index)]

    def core_copy(self, piece):
        return pltpu.make_async_remote_copy(
            src_ref=self.grads.at[1 - self.core, piece],
            dst_ref=self.core_in.at[piece],
            send_sem=self.send.at[piece, 0],
            recv_sem=self.recv.at[piece, 0],
            device_id=(self.tm, flip(self.patch, 1)),
            device_id_type=MESH,
        )

    def axis_copy(self, piece, stage, slot):
        axes, masks = self.order(piece)
        axis = axes[stage]
        here = self.coords[axis]
        where = (masks[0], 2, masks[1])[slot]
        mask = masks[1] if slot == 2 else masks[0]
        number = 1 + stage * 3 + slot
        return pltpu.make_async_remote_copy(
            src_ref=self.view(piece, stage, flip(here, where)),
            dst_ref=self.ins[stage].at[piece, slot],
            send_sem=self.send.at[piece, number],
            recv_sem=self.recv.at[piece, number],
            device_id=partner(self.tm, self.patch, axis, mask),
            device_id_type=MESH,
        )

    def steps(self):
        return 8

    def step(self, piece, number):
        if number == 0:
            self.core_copy(piece).start()
            return
        if number == 1:
            self.core_copy(piece).wait_recv()
            own = self.grads.at[self.core, piece]
            own[...] = own[...] + self.core_in[piece]
        else:
            stage, late = (number - 2) // 2, (number - 2) % 2
            axes, masks = self.order(piece)
            here = self.coords[axes[stage]]
            own = self.view(piece, stage, here)
            slots = self.ins[stage]
            if late == 0:
                self.axis_copy(piece, stage, 1).wait_recv()
                onward = self.view(piece, stage, flip(here, masks[1]))
                onward[...] = onward[...] + slots[piece, 1]
                self.axis_copy(piece, stage, 2).start()
                self.axis_copy(piece, stage, 0).wait_recv()
                own[...] = own[...] + slots[piece, 0]
                return
            self.axis_copy(piece, stage, 2).wait_recv()
            own[...] = own[...] + slots[piece, 2]
        stage = number // 2
        if stage < 3:
            self.axis_copy(piece, stage, 1).start()
            self.axis_copy(piece, stage, 0).start()

    def result(self, piece):
        x, y, z = self.coords
        return self.grads[self.core, piece, x, y, z]

    def finish(self, piece):
        self.core_copy(piece).wait_send()
        for stage in range(3):
            for slot in range(3):
                self.axis_copy(piece, stage, slot).wait_send()

    def neighbours(self):
        result = [(self.tm, flip(self.patch, 1))]
        for axis in range(3):
            for mask in (1, 3):
                result.append(partner(self.tm, self.patch, axis, mask))
        return result


F32, BF16 = jnp.float32, jnp.bfloat16
T = 256
D = 768
CHUNK = 256
CHUNKS = 3
SLOTS = 8
COLUMNS = 24
FACTOR = 1.0 / math.sqrt(128 * 256)
PIECES = 6


def split(value):
    high = value.astype(BF16)
    return high, (value - high.astype(F32)).astype(BF16)


def dot(a, b):
    return lax.dot_general(a, b, (((1,), (0,)), ((), ())), preferred_element_type=F32)


def dot_t(a, b):
    return lax.dot_general(a, b, (((1,), (1,)), ((), ())), preferred_element_type=F32)


def take(ref, c, rows):
    return jnp.concatenate([ref[2 * c, rows, :], ref[2 * c + 1, rows, :]], axis=1)


def put(ref, c, rows, value):
    ref[2 * c, rows, :] = value[:, :128]
    ref[2 * c + 1, rows, :] = value[:, 128:]


def regroup(src, dst, c):
    for lane in (2 * c, 2 * c + 1):
        for b in range(16):
            dst[lane, b * 16 : (b + 1) * 16, :] = src[lane, pl.ds(b, 16, stride=16), :]


def aligned(start, size, of):
    return pl.ds(pl.multiple_of(start, of), size)


def block_kernel(
    x_in, g_in, w_in, mixed_out, gi_out, gw_out,
    raw, l0, l1, xt, mid_home, mid_frame, gf, dmid_home, g_track, gi_home,
    staged, wh, wl, acts, spread, qn, kn, vn, qt, kt, probs, dt, do, dot_tr, bias,
    grads, core_in, in0, in1, in2,
    local_sem, stage_sem, tm_send, tm_recv, patch_send, patch_recv, rs_send, rs_recv, free_sem,
):
    tm, patch, core, coords = position()
    summing = ScatterSum(grads, core_in, (in0, in1, in2), rs_send, rs_recv)

    def tm_copy(src, dst, kind, c, d):
        other = flip(tm, d)
        return pltpu.make_async_remote_copy(
            src_ref=src.at[2 * c : 2 * c + 2, aligned(other * 32, 32, 32)],
            dst_ref=dst.at[2 * c : 2 * c + 2, aligned(tm * 32, 32, 32)],
            send_sem=tm_send.at[kind, c, d],
            recv_sem=tm_recv.at[kind, c, d],
            device_id=(other, patch),
            device_id_type=MESH,
        )

    def tm_start(src, dst, kind, c):
        for d in range(1, 8):
            tm_copy(src, dst, kind, c, d).start()
        own = aligned(tm * 32, 32, 32)
        for lane in (2 * c, 2 * c + 1):
            dst[lane, own, :] = src[lane, own, :]

    def tm_wait(src, dst, kind, c):
        for d in range(1, 8):
            tm_copy(src, dst, kind, c, d).wait_recv()

    def tm_sent(src, dst, kind, c):
        for d in range(1, 8):
            tm_copy(src, dst, kind, c, d).wait_send()

    def patch_copy(src, dst, kind, c, d):
        other = flip(patch, d)
        theirs, mine = aligned(other * 16, 16, 16), aligned(patch * 16, 16, 16)
        whole = len(src.shape) == 2
        return pltpu.make_async_remote_copy(
            src_ref=src.at[theirs] if whole else src.at[2 * c : 2 * c + 2, theirs],
            dst_ref=dst.at[mine] if whole else dst.at[2 * c : 2 * c + 2, mine],
            send_sem=patch_send.at[kind, c, d],
            recv_sem=patch_recv.at[kind, c, d],
            device_id=(tm, other),
            device_id_type=MESH,
        )

    def patch_start(src, dst, kind, c):
        for d in range(1, 16):
            patch_copy(src, dst, kind, c, d).start()
        if len(src.shape) == 3:
            own = aligned(patch * 16, 16, 16)
            for lane in (2 * c, 2 * c + 1):
                dst[lane, own, :] = src[lane, own, :]

    def patch_wait(src, dst, kind, c):
        for d in range(1, 16):
            patch_copy(src, dst, kind, c, d).wait_recv()

    def patch_sent(src, dst, kind, c):
        for d in range(1, 16):
            patch_copy(src, dst, kind, c, d).wait_send()

    def own_rows(src, dst, number):
        own = aligned(patch * 16, 16, 16)
        return pltpu.make_async_copy(src.at[own], dst.at[own], local_sem.at[number])

    def load(branch, k):
        slot = lax.rem(k, SLOTS)
        return pltpu.make_async_copy(
            w_in.at[branch, :, aligned(k * 128, 128, 128)], staged.at[slot], stage_sem.at[slot]
        )

    def prefetch(branch):
        for k in range(SLOTS):
            load(branch, k).start()

    def split_weights(branch, first, last):
        @pl.loop(first, last)
        def _(k):
            load(branch, k).wait()
            slot = lax.rem(k, SLOTS)
            lanes = aligned(k * 128, 128, 128)

            @pl.loop(0, 4)
            def _(r):
                rows = aligned(r * 192, 192, 64)
                high, low = split(staged[slot, rows, :])
                wh[rows, lanes] = high
                wl[rows, lanes] = low

            @pl.when(k + SLOTS < COLUMNS)
            def _():
                load(branch, k + SLOTS).start()

    def product(a, lanes):
        both = dot(a, wh[:, lanes])
        return both[:T] + both[T:] + dot(a[:T], wl[:, lanes])

    def normalize(branch, get):
        @pl.loop(0, 8)
        def _(r):
            rows = aligned(r * 32, 32, 32)
            parts = [get(c, rows) for c in range(CHUNKS)]
            total = parts[0] + parts[1] + parts[2]
            mean = jnp.sum(total, axis=1, keepdims=True) * (1.0 / D)
            parts = [part - mean for part in parts]
            square = parts[0] * parts[0] + parts[1] * parts[1] + parts[2] * parts[2]
            rstd = lax.rsqrt(jnp.sum(square, axis=1, keepdims=True) * (1.0 / D) + 1e-05)
            spread[branch, rows, :] = jnp.broadcast_to(rstd, (32, 128))
            for c in range(CHUNKS):
                high, low = split(parts[c] * rstd)
                acts[branch, 0, rows, c * CHUNK : (c + 1) * CHUNK] = high
                acts[branch, 0, aligned(T + r * 32, 32, 32), c * CHUNK : (c + 1) * CHUNK] = low

    def project(branch):
        normed = acts.at[branch, 0]

        def tile(i, base, scale):
            value = product(normed[...], aligned(base + i * 256, 256, 256))
            return value * scale if scale != 1.0 else value

        def natural(ref, lanes, value):
            high, low = split(value)
            ref[0:T, lanes] = high
            ref[T:, lanes] = low

        def turned(ref, i, value):
            high, low = split(value.T)
            rows = aligned(i * 256, 256, 256)
            ref[0, rows, :] = high
            ref[1, rows, :] = low

        @pl.loop(0, 3)
        def _(i):
            lanes = aligned(i * 256, 256, 256)
            value = tile(i, 0, 0.125)
            natural(qn, lanes, value)
            turned(qt.at[branch], i, value)

        @pl.loop(0, 3)
        def _(i):
            lanes = aligned(i * 256, 256, 256)
            value = tile(i, D, 1.0)
            natural(kn, lanes, value)
            turned(kt.at[branch], i, value)

        @pl.loop(0, 3)
        def _(i):
            natural(vn.at[branch], aligned(i * 256, 256, 256), tile(i, 2 * D, 1.0))

    def pair(ref, hp):
        lanes = aligned(hp * 128, 128, 128)
        return ref[0:T, lanes], ref[T:, lanes]

    def half_mask(e):
        lane = lax.broadcasted_iota(jnp.int32, (T, 128), 1)
        return jnp.where((lane >= 64) == (e == 1), 1.0, 0.0).astype(BF16)

    def inner(a, b, e):
        mask = half_mask(e)
        ah, al = a[0] * mask, a[1] * mask
        bh, bl = b
        return dot_t(
            jnp.concatenate([ah, al], axis=1), jnp.concatenate([bh, bh], axis=1)
        ) + dot_t(ah, bl)

    def probabilities(q, k, e, masked):
        scores = inner(q, k, e)
        if masked:
            scores = scores + bias[...]
        lifted = jnp.exp(scores - jnp.max(scores, axis=1, keepdims=True))
        return lifted * (1.0 / jnp.sum(lifted, axis=1, keepdims=True))

    def context(p, v):
        high, low = p
        both = dot(high, jnp.concatenate([v[0], v[1]], axis=1))
        return both[:, :128] + both[:, 128:] + dot(low, v[0])

    def store_context(branch, hp, values):
        lane = lax.broadcasted_iota(jnp.int32, (T, 128), 1)
        high, low = split(jnp.where(lane < 64, values[0], values[1]))
        lanes = aligned(hp * 128, 128, 128)
        acts[branch, 1, 0:T, lanes] = high
        acts[branch, 1, T:, lanes] = low

    def store_dt(start, value):
        high, low = split(value)
        rows = aligned(start, 64, 64)
        dt[0, rows, :] = high
        dt[1, rows, :] = low

    def head_back(branch, hp, e, p, ph, pw, v):
        dp = inner(pair(do, hp), v, e)
        ds = p * (dp - jnp.sum(dp * p, axis=1, keepdims=True))
        dsh, dsl = split(ds)
        start = hp * 128 + e * 64
        rows = aligned(start, 64, 64)

        def outer(ref, high, low, how):
            top = ref[0, rows, :]
            both = how(jnp.concatenate([top, ref[1, rows, :]], axis=0), high)
            return both[:64] + both[64:] + how(top, low)

        store_dt(start, outer(kt.at[branch], dsh, dsl, dot_t) * 0.125)
        store_dt(D + start, outer(qt.at[branch], dsh, dsl, dot))
        store_dt(2 * D + start, outer(dot_tr, ph, pw, dot))

    def out_gradient(get):
        for c in range(CHUNKS):
            value = get(c, slice(None))
            high, low = split(value)
            lanes = slice(c * CHUNK, (c + 1) * CHUNK)
            qn[0:T, lanes] = high
            qn[T:, lanes] = low
            high, low = split(value.T)
            rows = slice(3 * D + c * CHUNK, 3 * D + (c + 1) * CHUNK)
            dt[0, rows, :] = high
            dt[1, rows, :] = low

        @pl.loop(0, 3)
        def _(i):
            rows = aligned(i * 256, 256, 256)
            gh = qn[...]
            both = dot_t(gh, wh[rows, 3 * D :])
            value = both[:T] + both[T:] + dot_t(gh[:T], wl[rows, 3 * D :])
            high, low = split(value)
            do[0:T, rows] = high
            do[T:, rows] = low
            high, low = split(value.T)
            dot_tr[0, rows, :] = high
            dot_tr[1, rows, :] = low

    def back_to_normed():
        @pl.loop(0, CHUNKS)
        def _(c):
            rows = aligned(c * 256, 256, 256)
            value = (
                dot(wh[rows, : 3 * D], dt[0, : 3 * D, :])
                + dot(wh[rows, : 3 * D], dt[1, : 3 * D, :])
                + dot(wl[rows, : 3 * D], dt[0, : 3 * D, :])
            )
            put(l1, c, slice(None), value.T)

    def back_normalize(branch, get):
        @pl.loop(0, 8)
        def _(r):
            rows = aligned(r * 32, 32, 32)
            low_rows = aligned(T + r * 32, 32, 32)
            dn = [take(l1, c, rows) for c in range(CHUNKS)]
            n = [
                acts[branch, 0, rows, c * CHUNK : (c + 1) * CHUNK].astype(F32)
                + acts[branch, 0, low_rows, c * CHUNK : (c + 1) * CHUNK].astype(F32)
                for c in range(CHUNKS)
            ]
            mean = jnp.sum(dn[0] + dn[1] + dn[2], axis=1, keepdims=True) * (1.0 / D)
            along = dn[0] * n[0] + dn[1] * n[1] + dn[2] * n[2]
            along = jnp.sum(along, axis=1, keepdims=True) * (1.0 / D)
            rstd = spread[branch, rows, :][:, :1]
            for c in range(CHUNKS):
                put(l1, c, rows, get(c, rows) + rstd * (dn[c] - mean - n[c] * along))

    def weight_gradient(branch, c):
        lanes = slice(c * CHUNK, (c + 1) * CHUNK)

        @pl.loop(0, 4)
        def _(kind):
            rows = aligned(kind * D, D, D)
            source = kind // 3
            right_high = acts[branch, source, 0:T, lanes]
            right_low = acts[branch, source, T:, lanes]
            left = dt[0, rows, :]
            value = dot(left, right_high) + dot(left, right_low) + dot(dt[1, rows, :], right_high)
            for block in range(32):
                second, x_hi, y, half = block // 16, (block // 8) % 2, (block // 2) % 4, block % 2
                for lane in range(2):
                    grads[
                        half, 2 * c + lane, x_hi * 2 + kind // 2, y, 2 * lax.rem(kind, 2) + second
                    ] = value[block * 24 : block * 24 + 24, lane * 128 : (lane + 1) * 128]

    raw_loads = [
        pltpu.make_async_copy(
            x_in.at[:, lane * 128 : (lane + 1) * 128], raw.at[lane], local_sem.at[3 + lane]
        )
        for lane in range(2 * CHUNKS)
    ]
    for raw_load in raw_loads:
        raw_load.start()
    prefetch(0)
    g_own = own_rows(g_in, gf, 1)
    g_own.start()
    others = [(flip(tm, d), patch) for d in range(1, 8)]
    others += [(tm, flip(patch, d)) for d in range(1, 16)]
    others += [(flip(tm, 4), flip(patch, 8))]
    barrier = pltpu.get_barrier_semaphore()
    for other in others:
        pl.semaphore_signal(barrier, inc=1, device_id=other, device_id_type=MESH)
    row = (lax.broadcasted_iota(jnp.int32, (T, T), 0) // 16) % 2
    column = (lax.broadcasted_iota(jnp.int32, (T, T), 1) // 16) % 2
    bias[...] = jnp.where(row == column, 0.0, -1e30)
    for raw_load in raw_loads:
        raw_load.wait()
    for c in range(CHUNKS):
        regroup(raw, l0, c)
    pl.semaphore_wait(barrier, len(others))
    for c in range(CHUNKS):
        tm_start(l0, xt, 0, c)
    patch_start(g_in, gf, 0, 0)
    split_weights(0, 0, COLUMNS)
    prefetch(1)
    for c in range(CHUNKS):
        tm_wait(l0, xt, 0, c)

    normalize(0, lambda c, rows: take(xt, c, rows))
    project(0)

    @pl.loop(0, 6)
    def _(hp):
        q, k, v = pair(qn, hp), pair(kn, hp), pair(vn.at[0], hp)
        values = []
        for e in range(2):
            p = split(probabilities(q, k, e, True))
            probs[hp * 2 + e, 0] = p[0]
            probs[hp * 2 + e, 1] = p[1]
            values.append(context(p, v))
        store_context(0, hp, values)

    for c in range(CHUNKS):
        tm_sent(l0, xt, 0, c)
    for c in range(CHUNKS):
        value = product(acts[0, 1], pl.ds(3 * D + c * CHUNK, CHUNK))
        put(l1, c, slice(None), take(xt, c, slice(None)) + value)
        tm_start(l1, mid_home, 1, c)

    for c in range(CHUNKS):
        split_weights(1, c * 8, c * 8 + 8)
        tm_wait(l1, mid_home, 1, c)
        regroup(mid_home, l0, c)
        patch_start(l0, mid_frame, 1, c)
    prefetch(0)
    g_own.wait()
    patch_wait(g_in, gf, 0, 0)
    out_gradient(lambda c, rows: gf[rows, c * CHUNK : (c + 1) * CHUNK])
    for c in range(CHUNKS):
        patch_wait(l0, mid_frame, 1, c)

    normalize(1, lambda c, rows: take(mid_frame, c, rows))
    project(1)

    @pl.loop(0, 6)
    def _(hp):
        q, k, v = pair(qn, hp), pair(kn, hp), pair(vn.at[1], hp)
        values = []
        for e in range(2):
            p = probabilities(q, k, e, False)
            ph, pw = split(p)
            values.append(context((ph, pw), v))
            head_back(1, hp, e, p, ph, pw, v)
        store_context(1, hp, values)

    for c in range(CHUNKS):
        tm_sent(l1, mid_home, 1, c)
    back_to_normed()
    back_normalize(1, lambda c, rows: gf[rows, c * CHUNK : (c + 1) * CHUNK])
    for c in range(CHUNKS):
        patch_start(l1, dmid_home, 2, c)
    for c in range(CHUNKS):
        value = product(acts[1, 1], pl.ds(3 * D + c * CHUNK, CHUNK))
        gf[:, c * CHUNK : (c + 1) * CHUNK] = take(mid_frame, c, slice(None)) + value
    patch_start(gf, mixed_out, 3, 0)
    mixed_own = own_rows(gf, mixed_out, 2)
    mixed_own.start()

    for c in range(CHUNKS):
        patch_sent(l0, mid_frame, 1, c)
    for c in range(CHUNKS):
        weight_gradient(1, c)
        summing.step(2 * c, 0)
        summing.step(2 * c + 1, 0)
        patch_wait(l1, dmid_home, 2, c)
        regroup(dmid_home, l0, c)
        tm_start(l0, g_track, 2, c)
    def tick(number):
        for c in range(CHUNKS):
            if 1 <= number - c < summing.steps():
                for piece in (2 * c, 2 * c + 1):
                    summing.step(piece, number - c)

    split_weights(0, 0, 8)
    tick(1)
    split_weights(0, 8, 16)
    tick(2)
    split_weights(0, 16, 24)
    tick(3)
    for c in range(CHUNKS):
        tm_wait(l0, g_track, 2, c)

    out_gradient(lambda c, rows: take(g_track, c, rows))
    tick(4)

    def temporal_back(first, last):
        @pl.loop(first, last)
        def _(hp):
            v = pair(vn.at[0], hp)
            for e in range(2):
                ph, pw = probs[hp * 2 + e, 0], probs[hp * 2 + e, 1]
                head_back(0, hp, e, ph.astype(F32) + pw.astype(F32), ph, pw, v)

    temporal_back(0, 2)
    tick(5)
    temporal_back(2, 4)
    tick(6)
    temporal_back(4, 6)
    tick(7)
    tick(8)
    tick(9)
    for piece in range(PIECES):
        gw_out[1, :, piece * 128 : (piece + 1) * 128] = summing.result(piece) * FACTOR
        summing.finish(piece)
    for other in summing.neighbours():
        pl.semaphore_signal(free_sem, inc=1, device_id=other, device_id_type=MESH)
    for c in range(CHUNKS):
        weight_gradient(0, c)
        if c == 0:
            pl.semaphore_wait(free_sem, len(summing.neighbours()))
        summing.step(2 * c, 0)
        summing.step(2 * c + 1, 0)
    tick(1)
    for c in range(CHUNKS):
        patch_sent(l1, dmid_home, 2, c)
    back_to_normed()
    tick(2)
    back_normalize(0, lambda c, rows: take(g_track, c, rows))
    tick(3)
    for c in range(CHUNKS):
        tm_start(l1, gi_home, 3, c)
    tick(4)
    tick(5)
    for c in range(CHUNKS):
        tm_wait(l1, gi_home, 3, c)
        for lane in (2 * c, 2 * c + 1):
            for f in range(16):
                gi_out[f * 16 : (f + 1) * 16, lane * 128 : (lane + 1) * 128] = gi_home[
                    lane, pl.ds(f, 16, stride=16), :
                ]
    for number in range(6, 10):
        tick(number)
    for piece in range(PIECES):
        gw_out[0, :, piece * 128 : (piece + 1) * 128] = summing.result(piece) * FACTOR
        summing.finish(piece)

    patch_sent(g_in, gf, 0, 0)
    patch_sent(gf, mixed_out, 3, 0)
    patch_wait(gf, mixed_out, 3, 0)
    mixed_own.wait()
    for c in range(CHUNKS):
        tm_sent(l0, g_track, 2, c)
        tm_sent(l1, gi_home, 3, c)


def block(x, g, w):
    rows = pltpu.VMEM((T, D), F32)
    chunked = pltpu.VMEM((2 * CHUNKS, T, 128), F32)
    both = pltpu.VMEM((2 * T, D), BF16)
    turned = pltpu.VMEM((2, 2, D, T), BF16)
    scratch = dict(
        raw=chunked, l0=chunked, l1=chunked, xt=chunked, mid_home=chunked, mid_frame=chunked,
        gf=rows, dmid_home=chunked, g_track=chunked, gi_home=chunked,
        staged=pltpu.VMEM((SLOTS, D, 128), F32),
        wh=pltpu.VMEM((D, 4 * D), BF16),
        wl=pltpu.VMEM((D, 4 * D), BF16),
        acts=pltpu.VMEM((2, 2, 2 * T, D), BF16),
        spread=pltpu.VMEM((2, T, 128), F32),
        qn=both, kn=both,
        vn=pltpu.VMEM((2, 2 * T, D), BF16),
        qt=turned, kt=turned,
        probs=pltpu.VMEM((12, 2, T, T), BF16),
        dt=pltpu.VMEM((2, 4 * D, T), BF16),
        do=both,
        dot_tr=pltpu.VMEM((2, D, T), BF16),
        bias=pltpu.VMEM((T, T), F32),
        grads=pltpu.VMEM((2, PIECES, 4, 4, 4, 24, 128), F32),
        core_in=pltpu.VMEM((PIECES, 4, 4, 4, 24, 128), F32),
        in0=pltpu.VMEM((PIECES, 3, 4, 4, 24, 128), F32),
        in1=pltpu.VMEM((PIECES, 3, 4, 24, 128), F32),
        in2=pltpu.VMEM((PIECES, 3, 24, 128), F32),
        local_sem=pltpu.SemaphoreType.DMA((9,)),
        stage_sem=pltpu.SemaphoreType.DMA((SLOTS,)),
        tm_send=pltpu.SemaphoreType.DMA((4, 3, 8)),
        tm_recv=pltpu.SemaphoreType.DMA((4, 3, 8)),
        patch_send=pltpu.SemaphoreType.DMA((4, 3, 16)),
        patch_recv=pltpu.SemaphoreType.DMA((4, 3, 16)),
        rs_send=pltpu.SemaphoreType.DMA((PIECES, 10)),
        rs_recv=pltpu.SemaphoreType.DMA((PIECES, 10)),
        free_sem=pltpu.SemaphoreType.REGULAR,
    )
    anywhere = pl.BlockSpec(memory_space=pl.ANY)
    vmem = pl.BlockSpec(memory_space=pltpu.VMEM)
    return pl.pallas_call(
        block_kernel,
        out_shape=(
            jax.ShapeDtypeStruct((T, D), F32),
            jax.ShapeDtypeStruct((T, D), F32),
            jax.ShapeDtypeStruct((2, 24, D), F32),
        ),
        in_specs=[anywhere, anywhere, anywhere],
        out_specs=(anywhere, vmem, vmem),
        scratch_shapes=tuple(scratch.values()),
        compiler_params=pltpu.CompilerParams(
            collective_id=0, has_side_effects=True, vmem_limit_bytes=VMEM_LIMIT
        ),
    )(x, g, w)


def finish_kernel(*refs):
    copies = [pltpu.make_async_copy(refs[k], refs[3 + k], refs[6].at[k]) for k in range(3)]
    for copy in copies:
        copy.start()
    for copy in copies:
        copy.wait()


def finish(*results):
    anywhere = pl.BlockSpec(memory_space=pl.ANY)
    return pl.pallas_call(
        finish_kernel,
        out_shape=tuple(jax.ShapeDtypeStruct(r.shape, r.dtype) for r in results),
        in_specs=[anywhere] * 3,
        out_specs=(anywhere,) * 3,
        scratch_shapes=(pltpu.SemaphoreType.DMA((3,)),),
    )(*results)


def on_device(video_tokens, cotangent, weights):
    mixed, grad_input, summed = block(
        video_tokens.reshape(T, D), cotangent.reshape(T, D), weights
    )
    mixed, grad_input, grad_weights = finish(mixed, grad_input, summed)
    shape = video_tokens.shape
    return mixed.reshape(shape), grad_input.reshape(shape), grad_weights.transpose(0, 2, 1)


def solution(mesh):
    placed = (P("tm", "patch", None), P("tm", "patch", None), P())
    return jax.shard_map(
        on_device,
        mesh=mesh,
        in_specs=placed,
        out_specs=(P("tm", "patch", None), P("tm", "patch", None), P(None, None, ("tm", "patch"))),
        check_vma=False,
    )
```

time: 555 us -> 272 us (0.49)
  the two profiles are of different devices: /device:TPU:1 before, /device:TPU:8 now
where the time goes in v1:
time: 272 us
  Pallas kernels  271 us (100%)
    pallas_call x1, Pallas kernels, block(): pl.pallas_call(block_kernel, out_shape=(jax.ShapeDtypeStruct((T, D), F32)...  218 us
    pallas_call x1, Pallas kernels, finish(): pl.pallas_call(finish_kernel, out_shape=tuple((jax.ShapeDtypeStruct(r.sha...  53.2 us

profile of v1, /device:TPU:8, one launch (start us, length us, event | category | flops | bytes accessed | tf_op | source)
XLA Modules:
  0.0 272.1 jit_solution(7137100997171387550)
XLA Ops:
  0.6 218.1 %shard_map.58 = (f32[256,768]{1,0:T(8,128)}, f32[256,768]{1,0:T(8,128)}, f32[2,24,768]{2,1,0:T(8,128)}) custom-call(f32[256,768]{1,0:T(8,128)} %bitcast.5, f32[256,768]{1,0:T(8,128)} %bitcast.6, f32[2,768,3072]{2,1,0:T(8,128)} %w_in.1), custom_call_target="tpu_custom_call" | custom-call | tf_op jit(solution)/shard_map/pallas_call | solution.py:679
  218.7 53.2 %shard_map.59 = (f32[256,768]{1,0:T(8,128)}, f32[256,768]{1,0:T(8,128)}, f32[2,24,768]{2,1,0:T(8,128)}) custom-call(f32[256,768]{1,0:T(8,128)} %get-tuple-element.9.refs_0_, f32[256,768]{1,0:T(8,128)} %get-tuple-element.10.refs_1_, f32[2,24,768]{2,1,0:T(8,128)} %get-tuple-element.11.refs_2_), custom_call_target="tpu_custom_call" | custom-call | tf_op jit(solution)/shard_map/pallas_call | solution.py:705
